TPU v7x, 32 devices: a whole 2x2x4 slice. The times are simulated.
32 devices in a mesh: row: 8 (over y, x, core), col: 4 (over z).
Axes of the slice: x: 2, y: 2, z: 4, core: 2. Of those that a mesh axis runs over, the one named last changes fastest.
Arguments:
- amplitudes: bfloat16 [1280, 3, 256], P(('row', 'col')), may hold values from -6 to 6
- integrals: bfloat16 [3, 256, 65536], P(None, 'row', 'col'), may hold values from -0.625 to 0.625
- pair_irrep: int32 [3, 256], replicated, may hold values from 0 to 8
- block_offset: int32 [9], replicated, may hold values from 0 to 65536, as said below
- residual: bfloat16 [1280, 65536], P(('row', 'col')), may hold values from -6 to 6
Outputs:
- residual_out: bfloat16 [1280, 65536], P(('row', 'col'))
Inputs may be any that keep to these rules, and one draw needn't show every extreme that they name: block_offset[0] is 0 and block_offset[8] is 65536; the entries rise strictly and are multiples of 128.
All inputs are finite; a program needn't handle non-finite values.
Results may differ from a plain program's by a relative error of at most 0.0043.
Values may be sent and summed in bfloat16 or wider, within the bound.
A program may use at most 192 MiB of HBM per device.

v0:
```python
import jax
import jax.numpy as jnp
from jax import lax
from jax.sharding import PartitionSpec as P


def apply_piece(irrep_ab, amp_panel, labels, total, piece):
    kept = jnp.where(labels[:, None] == irrep_ab[None, :], piece, jnp.zeros((), piece.dtype))
    return total + jnp.dot(amp_panel, kept, preferred_element_type=jnp.float32)


def per_device(amplitudes, integrals, pair_irrep, block_offset, residual):
    ab_local = integrals.shape[2]
    steps = integrals.shape[0]
    position = lax.axis_index("col") * ab_local + lax.iota(jnp.int32, ab_local)
    irrep_ab = jnp.sum((position[:, None] >= block_offset[None, 1:-1]).astype(jnp.int32), axis=1)
    grid_amps = lax.all_to_all(amplitudes, "col", split_axis=2, concat_axis=0, tiled=True)
    panels = [
        lax.all_gather(grid_amps[:, step, :], "col", axis=1, tiled=True) for step in range(steps)
    ]
    empty = jnp.zeros((panels[0].shape[0], ab_local), jnp.float32)
    total = empty
    piece = lax.all_gather(integrals, "row", axis=1, tiled=True)
    for step in range(steps):
        total = apply_piece(irrep_ab, panels[step], pair_irrep[step], total, piece[step])
    ladder_half = total.astype(jnp.bfloat16)
    returned = lax.all_to_all(ladder_half, "col", split_axis=0, concat_axis=1, tiled=True)
    return (residual.astype(jnp.float32) + returned.astype(jnp.float32)).astype(jnp.bfloat16)


def solution(mesh):
    in_specs = (
        P(("row", "col"), None, None),
        P(None, "row", "col"),
        P(),
        P(),
        P(("row", "col"), None),
    )
    out_specs = P(("row", "col"), None)
    return jax.shard_map(
        per_device, mesh=mesh, in_specs=in_specs, out_specs=out_specs, check_vma=False
    )
```

profile of v0, /device:TPU:0, one launch (start us, length us, event | category | flops | bytes accessed | tf_op | source)
XLA Modules:
  0.0 308.5 jit_solution(6142728885704960795)
XLA Ops:
  6.5 0.0 all-gather.5.cloned.1.call-start
  6.5 0.7 all-gather.5.cloned.1.call-update
  7.3 1.0 copy.18
  8.3 0.9 reshape.18
  9.2 6.3 %all-to-all-start = ((bf16[4,2,3840]{2,1,0:T(2,128)(2,1)}), bf16[4,2,3840]{2,1,0:T(2,128)(2,1)S(1)}, u32[]{:S(2)}, u32[]{:S(2)}) async-start(bf16[4,2,3840]{2,1,0:T(2,128)(2,1)} %reshape.18), calls=%async_computation | async-start | bytes 122880 | tf_op jit(solution)/shard_map/all_to_all | solution.py:17
  15.5 0.7 slice.31
  16.3 0.8 fusion.18
  17.1 0.2 convert_reduce_fusion
  17.3 3.9 %all-to-all-done = bf16[4,2,3840]{2,1,0:T(2,128)(2,1)S(1)} async-done(((bf16[4,2,3840]{2,1,0:T(2,128)(2,1)}), bf16[4,2,3840]{2,1,0:T(2,128)(2,1)S(1)}, u32[]{:S(2)}, u32[]{:S(2)}) %all-to-all-start) | async-done | bytes 61472 | tf_op jit(solution)/shard_map/all_to_all | solution.py:17
  21.3 0.3 reshape.19
  21.6 0.2 copy.19
  21.8 0.1 copy.24
  21.9 0.1 copy.22
  22.0 0.1 copy.20
  22.1 13.3 %all-gather = bf16[160,1,256]{0,2,1:T(8,128)(2,1)S(1)} all-gather(bf16[160,1,64]{0,2,1:T(8,128)(2,1)S(1)} %copy.20), channel_id=2, replica_groups=mesh['row'=8,'col'=4] {'col'}, dimensions={2}, use_global_device_ids=true | all-gather | bytes 102400 | tf_op jit(solution)/shard_map/all_gather | solution.py:19
  35.4 13.6 %all-gather.1 = bf16[160,1,256]{0,2,1:T(8,128)(2,1)S(1)} all-gather(bf16[160,1,64]{0,2,1:T(8,128)(2,1)S(1)} %copy.22), channel_id=3, replica_groups=mesh['row'=8,'col'=4] {'col'}, dimensions={2}, use_global_device_ids=true | all-gather | bytes 102400 | tf_op jit(solution)/shard_map/all_gather | solution.py:19
  49.0 13.3 %all-gather.2 = bf16[160,1,256]{0,2,1:T(8,128)(2,1)S(1)} all-gather(bf16[160,1,64]{0,2,1:T(8,128)(2,1)S(1)} %copy.24), channel_id=4, replica_groups=mesh['row'=8,'col'=4] {'col'}, dimensions={2}, use_global_device_ids=true | all-gather | bytes 102400 | tf_op jit(solution)/shard_map/all_gather | solution.py:19
  62.4 75.0 %all-gather.5.cloned.1.call-done = bf16[3,256,16384]{2,1,0:T(8,128)(2,1)} async-done(((bf16[3,32,16384]{2,1,0:T(8,128)(2,1)}), bf16[3,256,16384]{2,1,0:T(8,128)(2,1)}) %all-gather.5.cloned.1.call-update) | async-done | bytes 25165840 | tf_op jit(solution)/shard_map/all_gather | solution.py:23
  137.3 10.3 %fusion.1 = f32[16384,160]{0,1:T(8,128)} fusion(bf16[3,256,16384]{2,1,0:T(8,128)(2,1)} %all-gather.5.cloned.1.call-done, s32[16384]{0:T(1024)S(1)} %convert_reduce_fusion, s32[256]{0:T(256)S(1)} %bitcast.50, bf16[160,1,256]{0,2,1:T(8,128)(2,1)S(1)} %all-gather), kind=kOutput, calls=%fused_computation.8 | convolution fusion | flops 1350565888 | bytes 19022848 | tf_op jit(solution)/shard_map/dot_general | solution.py:9
  147.6 9.7 %convolution_add_fusion.1 = f32[16384,160]{0,1:T(8,128)S(1)} fusion(f32[16384,160]{0,1:T(8,128)} %fusion.1, bf16[3,256,16384]{2,1,0:T(8,128)(2,1)} %all-gather.5.cloned.1.call-done, s32[16384]{0:T(1024)S(1)} %convert_reduce_fusion, s32[256]{0:T(256)S(1)} %bitcast.48, bf16[160,1,256]{0,2,1:T(8,128)(2,1)S(1)} %all-gather.1), kind=kOutput, calls=%fused_computation.1 | convolution fusion | flops 1353187328 | bytes 29508608 | tf_op jit(solution)/shard_map/dot_general | solution.py:9
  157.4 9.2 %fusion = bf16[16384,160]{0,1:T(8,128)(2,1)} fusion(f32[16384,160]{0,1:T(8,128)S(1)} %convolution_add_fusion.1, bf16[3,256,16384]{2,1,0:T(8,128)(2,1)} %all-gather.5.cloned.1.call-done, s32[16384]{0:T(1024)S(1)} %convert_reduce_fusion, s32[256]{0:T(256)S(1)} %bitcast.49, bf16[160,1,256]{0,2,1:T(8,128)(2,1)S(1)} %all-gather.2), kind=kOutput, calls=%fused_computation.2 | convolution fusion | flops 1355808768 | bytes 24265728 | tf_op jit(solution)/shard_map/dot_general | solution.py:9
  166.6 120.6 %all_to_all.31 = bf16[4,40,16384]{2,1,0:T(8,128)(2,1)S(1)} all-to-all(bf16[4,40,16384]{2,1,0:T(8,128)(2,1)} %bitcast.44), channel_id=1, replica_groups=mesh['row'=8,'col'=4] {'col'}, dimensions={0} | all-to-all | bytes 10485760 | tf_op jit(solution)/shard_map/all_to_all | solution.py:27
  287.2 1.1 convert_bitcast_fusion
  288.4 4.7 %copy.27 = f32[4,5,8,16384]{3,2,0,1:T(8,128)} copy(f32[4,5,8,16384]{3,2,1,0:T(8,128)S(1)} %convert_bitcast_fusion) | data formatting | bytes 20971520 | tf_op jit(solution)/shard_map/convert_element_type | solution.py:28
  293.0 8.7 %add_convert_fusion = bf16[40,65536]{1,0:T(8,128)(2,1)} fusion(f32[40,65536]{1,0:T(8,128)} %bitcast.43, bf16[40,65536]{1,0:T(8,128)(2,1)} %param.9), kind=kLoop, calls=%fused_computation.7 | loop fusion | flops 7864320 | bytes 20971520 | tf_op jit(solution)/shard_map/convert_element_type | solution.py:28
  (2 shorter events, 0.0 us)
Async XLA Ops:
  6.5 130.8 %all-gather.5.cloned.1.call-start = ((), (), s32[]{:S(2)}) async-start(), calls=%async_computation.2 | async-start | bytes 28311552 | tf_op jit(solution)/shard_map/all_gather | solution.py:23
  9.2 12.1 %all-to-all-start = ((bf16[4,2,3840]{2,1,0:T(2,128)(2,1)}), bf16[4,2,3840]{2,1,0:T(2,128)(2,1)S(1)}, u32[]{:S(2)}, u32[]{:S(2)}) async-start(bf16[4,2,3840]{2,1,0:T(2,128)(2,1)} %reshape.18), calls=%async_computation | async-start | bytes 122880 | tf_op jit(solution)/shard_map/all_to_all | solution.py:17
Sparse Core Ops, SparseCore 0:
  9.3 128.0 all-gather.4
where the time goes:
time: 309 us
  blocking collectives  161 us (52%)
  waiting for transfers between devices  79.6 us (26%)
  matrix products  29.3 us (9%)
  between operations  13.5 us (4%)
  other arithmetic  10.1 us (3%)
  local copies, waits for them, and re-layouts  8.94 us (3%)
  starting transfers between devices  6.32 us (2%)
    all_to_all x1, blocking collectives, per_device(): lax.all_to_all(ladder_half, 'col', split_axis=0, concat_axis=1, tiled=True)  121 us
    all_gather x1, waiting for transfers between devices, per_device(): piece = lax.all_gather(integrals, 'row', axis=1, tiled=True)  75 us
    all_gather x3, blocking collectives, per_device(): lax.all_gather(grid_amps[:, step, :], 'col', axis=1, tiled=True)  40.3 us
    dot_general x3, matrix products, apply_piece(): return total + jnp.dot(amp_panel, kept, preferred_element_type=jnp.float32)  29.3 us
    convert_element_type x1, other arithmetic, per_device(): (residual.astype(jnp.float32) + returned.astype(jnp.float32)).astype(jnp....  8.67 us
    all_to_all x1, starting transfers between devices, per_device(): lax.all_to_all(amplitudes, 'col', split_axis=2, concat_axis=0, tiled=True)  6.32 us
  transfers between devices with their start and end apart: 2, of which 2 were waited for; matrix products, arithmetic and copies ran while one was open for 1% of the time, Pallas kernels for 0%

commit v1 on v0

v1 whole, which is shorter than its diff:
```python
import functools

import jax
import jax.numpy as jnp
from jax import lax
from jax.experimental import pallas as pl
from jax.experimental.pallas import tpu as pltpu
from jax.sharding import PartitionSpec as P

NIRREP = 8
GRAIN = 128
MIB = 1024 * 1024


def apply_piece(irrep_ab, amp_panel, labels, total, piece):
    kept = jnp.where(labels[:, None] == irrep_ab[None, :], piece, jnp.zeros((), piece.dtype))
    return total + jnp.dot(amp_panel, kept, preferred_element_type=jnp.float32)


def dense(amplitudes, integrals, pair_irrep, block_offset, residual):
    ab_local = integrals.shape[2]
    steps = integrals.shape[0]
    position = lax.axis_index("col") * ab_local + lax.iota(jnp.int32, ab_local)
    irrep_ab = jnp.sum((position[:, None] >= block_offset[None, 1:-1]).astype(jnp.int32), axis=1)
    grid_amps = lax.all_to_all(amplitudes, "col", split_axis=2, concat_axis=0, tiled=True)
    panels = [
        lax.all_gather(grid_amps[:, step, :], "col", axis=1, tiled=True) for step in range(steps)
    ]
    total = jnp.zeros((panels[0].shape[0], ab_local), jnp.float32)
    piece = lax.all_gather(integrals, "row", axis=1, tiled=True)
    for step in range(steps):
        total = apply_piece(irrep_ab, panels[step], pair_irrep[step], total, piece[step])
    ladder_half = total.astype(jnp.bfloat16)
    returned = lax.all_to_all(ladder_half, "col", split_axis=0, concat_axis=1, tiled=True)
    return (residual.astype(jnp.float32) + returned.astype(jnp.float32)).astype(jnp.bfloat16)


def round_up(value, grain):
    return (value + grain - 1) // grain * grain


def one_hot_rows(slot_ref, g, rows):
    width = slot_ref.shape[1]
    line = slot_ref[pl.ds(g, 1), :]
    at = lax.broadcasted_iota(jnp.int32, (rows, width), 0)
    return jnp.where(line == at, 1.0, 0.0).astype(jnp.bfloat16)


def pack_kernel(irrep_ref, slot_ref, x_ref, out_ref, pick, *, blocks, per_step):
    rows = pick.shape[1]

    @pl.when(pl.program_id(0) == 0)
    def _():
        for g in range(NIRREP):
            pick[g] = one_hot_rows(slot_ref, g, rows)

    x = x_ref[...].reshape(-1, x_ref.shape[-1])
    first = irrep_ref[blocks] + pl.program_id(0) * per_step
    for t in range(per_step):
        g = irrep_ref[first + t]
        cols = slice(t * GRAIN, (t + 1) * GRAIN)
        packed = jnp.dot(pick[g], x[:, cols], preferred_element_type=jnp.float32)
        out_ref[0, :, cols] = packed.astype(jnp.bfloat16)


def pack(x, slot, irrep_blk, first, rows, parts):
    width = x.shape[-1] // parts
    depth = slot.shape[1]
    blocks = irrep_blk.shape[0]
    scalars = jnp.concatenate([irrep_blk, first[None].astype(jnp.int32)])
    lead = x.ndim - 1
    return pl.pallas_call(
        functools.partial(pack_kernel, blocks=blocks, per_step=width // GRAIN),
        out_shape=jax.ShapeDtypeStruct((parts, rows, width), jnp.bfloat16),
        grid_spec=pltpu.PrefetchScalarGridSpec(
            num_scalar_prefetch=1,
            grid=(parts,),
            in_specs=[
                pl.BlockSpec((NIRREP, depth), lambda i, s: (0, 0)),
                pl.BlockSpec(x.shape[:-1] + (width,), lambda i, s: (0,) * lead + (i,)),
            ],
            out_specs=pl.BlockSpec((1, rows, width), lambda i, s: (i, 0, 0)),
            scratch_shapes=[pltpu.VMEM((NIRREP, rows, depth), jnp.bfloat16)],
        ),
        compiler_params=pltpu.CompilerParams(vmem_limit_bytes=24 * MIB),
    )(scalars, slot, x)


def ladder_kernel(irrep_ref, slot_ref, amp_ref, packed_ref, res_ref, out_ref, amps, *, per_step):
    rows = amps.shape[2]

    @pl.when(pl.program_id(0) == 0)
    def _():
        for g in range(NIRREP):
            pick = one_hot_rows(slot_ref, g, rows)
            amps[g] = lax.dot_general(
                amp_ref[...], pick, (((1,), (1,)), ((), ())), preferred_element_type=jnp.float32
            ).astype(jnp.bfloat16)

    first = pl.program_id(0) * per_step
    for t in range(per_step):
        g = irrep_ref[first + t]
        cols = slice(t * GRAIN, (t + 1) * GRAIN)
        ladder = jnp.dot(amps[g], packed_ref[0, :, cols], preferred_element_type=jnp.float32)
        ladder = ladder.astype(jnp.bfloat16).astype(jnp.float32)
        out_ref[:, cols] = (res_ref[:, cols].astype(jnp.float32) + ladder).astype(jnp.bfloat16)


def ladder_add(amp, slot, irrep_blk, packed, residual, n_row, n_col):
    parts, rows, width = packed.shape
    pairs, depth = amp.shape
    return pl.pallas_call(
        functools.partial(ladder_kernel, per_step=width // GRAIN),
        out_shape=jax.ShapeDtypeStruct(residual.shape, jnp.bfloat16),
        grid_spec=pltpu.PrefetchScalarGridSpec(
            num_scalar_prefetch=1,
            grid=(parts,),
            in_specs=[
                pl.BlockSpec((NIRREP, depth), lambda i, s: (0, 0)),
                pl.BlockSpec((pairs, depth), lambda i, s: (0, 0)),
                pl.BlockSpec((1, rows, width), lambda i, s: ((i % n_row) * n_col + i // n_row, 0, 0)),
                pl.BlockSpec((pairs, width), lambda i, s: (0, i)),
            ],
            out_specs=pl.BlockSpec((pairs, width), lambda i, s: (0, i)),
            scratch_shapes=[pltpu.VMEM((NIRREP, pairs, rows), jnp.bfloat16)],
        ),
        compiler_params=pltpu.CompilerParams(vmem_limit_bytes=24 * MIB),
    )(irrep_blk, slot, amp, packed, residual)


def per_device(n_row, n_col, amplitudes, integrals, pair_irrep, block_offset, residual):
    steps, local_k, ab_local = integrals.shape
    n1 = steps * local_k
    cap1 = round_up(-(-n1 // 3), 16)
    cap2 = round_up(-(-n1 * n_row // 6), 16)
    row, col = lax.axis_index("row"), lax.axis_index("col")

    labels = pair_irrep.reshape(steps, n_row, local_k).transpose(1, 0, 2).reshape(n_row, n1)
    irreps = lax.iota(jnp.int32, NIRREP)
    mine = labels[None] == irreps[:, None, None]
    running = jnp.cumsum(mine.astype(jnp.int32), axis=2)
    count = running[:, :, -1]
    rank = jnp.where(mine, running - 1, -1)
    upto = jnp.cumsum(count, axis=1)
    base = upto - count
    fits = (jnp.max(count) <= cap1) & (jnp.max(upto) <= cap2)

    slot1 = lax.dynamic_index_in_dim(rank, row, axis=1, keepdims=False)
    spot = lax.iota(jnp.int32, cap1)
    slot2 = jnp.where(spot[None, None] < count[:, :, None], base[:, :, None] + spot, -1)
    slot2 = slot2.reshape(NIRREP, n_row * cap1)
    slot3 = jnp.where(mine, base[:, :, None] + rank, -1)
    slot3 = slot3.reshape(NIRREP, n_row, steps, local_k).transpose(0, 2, 1, 3).reshape(NIRREP, -1)

    blocks = n_col * ab_local // GRAIN
    starts = lax.iota(jnp.int32, blocks) * GRAIN
    irrep_blk = jnp.sum((starts[:, None] >= block_offset[None, 1:-1]).astype(jnp.int32), axis=1)

    def sparse(amplitudes, integrals, residual):
        per_col = ab_local // GRAIN
        mine1 = pack(integrals, slot1, irrep_blk, col * per_col, cap1, n_row)
        ours = lax.all_to_all(mine1, "row", split_axis=0, concat_axis=0, tiled=True)
        ours = ours.reshape(n_row * cap1, ab_local // n_row)
        first = col * per_col + row * (per_col // n_row)
        mine2 = pack(ours, slot2, irrep_blk, first, cap2, 1)
        packed = lax.all_gather(mine2, ("row", "col"), axis=0, tiled=True)
        amp = amplitudes.reshape(amplitudes.shape[0], -1)
        return ladder_add(amp, slot3, irrep_blk, packed, residual, n_row, n_col)

    def full(amplitudes, integrals, residual):
        return dense(amplitudes, integrals, pair_irrep, block_offset, residual)

    return lax.cond(fits, sparse, full, amplitudes, integrals, residual)


def solution(mesh):
    in_specs = (
        P(("row", "col"), None, None),
        P(None, "row", "col"),
        P(),
        P(),
        P(("row", "col"), None),
    )
    out_specs = P(("row", "col"), None)
    body = functools.partial(per_device, mesh.shape["row"], mesh.shape["col"])
    return jax.shard_map(
        body, mesh=mesh, in_specs=in_specs, out_specs=out_specs, check_vma=False
    )
```

time: 309 us -> 194 us (0.63)
  blocking collectives: 161 us -> 0 us
  waiting for transfers between devices: 79.6 us -> 128 us
  Pallas kernels: 0 us -> 32.1 us
  matrix products: 29.3 us -> 0 us
  other arithmetic: 10.1 us -> 3.25 us
    all_to_all x1 -> x0, blocking collectives: 121 us -> none  [per_device(): lax.all_to_all(ladder_half, 'col', split_axis=0, concat_axis=1, tiled=True)]
    all_gather x3 -> x0, blocking collectives: 40.3 us -> none  [per_device(): lax.all_gather(grid_amps[:, step, :], 'col', axis=1, tiled=True)]
    all_gather x1, waiting for transfers between devices: 75 us -> 114 us  [sparse(): packed = lax.all_gather(mine2, ('row', 'col'), axis=0, tiled=True)]
    pallas_call x0 -> x3, Pallas kernels: none -> 32.1 us  [the longest x1 23.2 us: ladder_add(): pl.pallas_call(functools.partial(ladder_kernel, per_step=width // GRAIN),...]
    dot_general x3 -> x0, matrix products: 29.3 us -> none  [apply_piece(): return total + jnp.dot(amp_panel, kept, preferred_element_type=jnp.float32)]
    all_to_all x1, waiting for transfers between devices: 3.95 us -> 14.8 us  [sparse(): ours = lax.all_to_all(mine1, 'row', split_axis=0, concat_axis=0, tiled=True)]
    convert_element_type x1, other arithmetic: 8.67 us -> 0.07 us  [per_device(): (starts[:, None] >= block_offset[None, 1:-1]).astype(jnp.int32)]
    cond x0 -> x2, local copies, waits for them, and re-layouts: none -> 5.77 us
where the time goes in v1:
time: 194 us; the launch traced here: 193 us
  waiting for transfers between devices  128 us (66%)
  Pallas kernels  32.1 us (17%)
  between operations  14.8 us (8%)
  local copies, waits for them, and re-layouts  9.06 us (5%)
  starting transfers between devices  5.21 us (3%)
  other arithmetic  3.25 us (2%)
    all_gather x1, waiting for transfers between devices, sparse(): packed = lax.all_gather(mine2, ('row', 'col'), axis=0, tiled=True)  114 us
    pallas_call x1, Pallas kernels, ladder_add(): pl.pallas_call(functools.partial(ladder_kernel, per_step=width // GRAIN),...  23.2 us
    all_to_all x1, waiting for transfers between devices, sparse(): ours = lax.all_to_all(mine1, 'row', split_axis=0, concat_axis=0, tiled=True)  14.8 us
    pallas_call x2, Pallas kernels, pack(): pl.pallas_call(functools.partial(pack_kernel, blocks=blocks, per_step=wid...  8.95 us
    cond x2, local copies, waits for them, and re-layouts  5.77 us
    all_to_all x1, starting transfers between devices, sparse(): ours = lax.all_to_all(mine1, 'row', split_axis=0, concat_axis=0, tiled=True)  5.17 us
  transfers between devices with their start and end apart: 2, of which 2 were waited for; matrix products, arithmetic and copies ran while one was open for 1% of the time, Pallas kernels for 0%

profile of v1, /device:TPU:0, one launch (start us, length us, event | category | flops | bytes accessed | tf_op | source)
XLA Modules:
  0.0 192.8 jit_solution(10601833807573260822)
XLA Ops:
  6.5 0.7 slice.37
  7.3 0.8 reshape.50
  8.0 0.1 eq.63
  8.1 0.1 compare_convert_fusion
  8.2 2.0 %reduce_window_sum.22 = s32[8,8,96]{2,1,0:T(8,128)S(1)} reduce-window(s32[8,8,96]{2,1,0:T(8,128)S(1)} %copy.50, s32[]{:T(128)} %constant.44.clone.1), window={size=1x1x96 pad=0_0x0_0x95_0}, to_apply=%region_0.0 | reduce-window | flops 583680 | bytes 49156 | tf_op jit(solution)/shard_map/jit(cumsum)/reduce_window_sum | solution.py:141
  10.2 0.1 slice.44
  10.4 0.9 subtract_reduce_fusion
  12.6 0.1 sub.14
  12.8 0.1 select_bitcast_fusion
  12.9 173.0 %conditional.1 = (bf16[40,65536]{1,0:T(8,128)(2,1)}) conditional(s32[]{:T(128)} %convert_element_type.34, (bf16[40,65536]{1,0:T(8,128)(2,1)}, s32[3,256]{1,0:T(4,128)}, s32[9]{0:T(128)}, bf16[3,32,16384]{2,1,0:T(8,128)(2,1)}, bf16[40,3,256]{2,0,1:T(8,128)(2,1)}) %tuple.15, (s32[512,7]{0,1:T(8,128)S(1)}, s32[8,3,8,32]{3,1,2,0:T(4,128)S(1)}, ...), branch_computations={%region_4.6_spmd, %region_6.8_spmd} | conditional | flops 4070391808 | bytes 227321024 | solution.py:173
  13.0 7.0 %branch_1_fun.3 = bf16[8,32,2048]{2,1,0:T(8,128)(2,1)} custom-call(s32[513]{0:T(1024)S(1)} %get-tuple-element.170.irrep_ref, s32[8,96]{1,0:T(8,128)S(1)} %fusion.18.slot_ref, bf16[3,32,16384]{2,1,0:T(8,128)(2,1)} %get-tuple-element.91.x_ref), custom_call_target="tpu_custom_call" | custom-call | tf_op jit(solution)/shard_map/cond/branch_1_fun/pallas_call | solution.py:72
  20.0 5.2 %all-to-all-start = ((bf16[8,32,2048]{2,1,0:T(8,128)(2,1)}), bf16[8,32,2048]{2,1,0:T(8,128)(2,1)S(1)}, u32[]{:S(2)}, u32[]{:S(2)}) async-start(bf16[8,32,2048]{2,1,0:T(8,128)(2,1)} %branch_1_fun.3), calls=%async_computation | async-start | bytes 2097152 | tf_op jit(solution)/shard_map/cond/branch_1_fun/all_to_all | solution.py:162
  25.2 0.0 all-gather.8.cloned.1.call-start
  25.2 0.1 lt.30
  25.3 0.1 lt.24
  25.4 0.1 copy.54
  25.5 0.1 lt.27
  25.6 0.1 lt.28
  25.6 0.1 add.52
  25.7 0.1 add.53
  25.8 14.8 %all-to-all-done = bf16[8,32,2048]{2,1,0:T(8,128)(2,1)S(1)} async-done(((bf16[8,32,2048]{2,1,0:T(8,128)(2,1)}), bf16[8,32,2048]{2,1,0:T(8,128)(2,1)S(1)}, u32[]{:S(2)}, u32[]{:S(2)}) %all-to-all-start) | async-done | bytes 1048608 | tf_op jit(solution)/shard_map/cond/branch_1_fun/all_to_all | solution.py:162
  40.6 2.0 %branch_1_fun.4 = bf16[1,128,2048]{2,1,0:T(8,128)(2,1)} custom-call(s32[513]{0:T(1024)S(1)} %get-tuple-element.171.irrep_ref, s32[8,256]{1,0:T(8,128)S(1)} %add_select_fusion.slot_ref, bf16[256,2048]{1,0:T(8,128)(2,1)S(1)} %bitcast.59), custom_call_target="tpu_custom_call" | custom-call | tf_op jit(solution)/shard_map/cond/branch_1_fun/pallas_call | solution.py:72
  42.5 0.0 all-gather.8.cloned.1.call-update
  42.6 0.8 copy.59
  43.4 0.1 reshape.46.slot_ref
  43.5 113.5 %all-gather.8.cloned.1.call-done.packed_ref = bf16[32,128,2048]{2,1,0:T(8,128)(2,1)} async-done(((bf16[1,128,2048]{2,1,0:T(8,128)(2,1)}), bf16[32,128,2048]{2,1,0:T(8,128)(2,1)}) %all-gather.8.cloned.1.call-update) | async-done | bytes 16777232 | tf_op jit(solution)/shard_map/cond/branch_1_fun/all_gather | solution.py:166
  157.0 0.0 copy-start
  157.0 5.8 %copy-done = bf16[32,128,2048]{2,1,0:T(8,128)(2,1)S(1)} copy-done((bf16[32,128,2048]{2,1,0:T(8,128)(2,1)S(1)}, bf16[32,128,2048]{2,1,0:T(8,128)(2,1)}, u32[]{:S(2)}) %copy-start) | copy-done | bytes 16777240 | tf_op jit(solution)/shard_map/cond
  162.8 23.2 %branch_1_fun.5 = bf16[40,65536]{1,0:T(8,128)(2,1)} custom-call(s32[512]{0:T(512)S(1)} %reduce_sum.18.irrep_ref, s32[8,768]{1,0:T(8,128)S(1)} %reshape.46.slot_ref, bf16[40,768]{1,0:T(8,128)(2,1)S(1)} %bitcast.60, bf16[32,128,2048]{2,1,0:T(8,128)(2,1)S(1)} %copy-done, bf16[40,65536]{1,0:T(8,128)(2,1)} %get-tuple-element.92.res_ref), custom_call_target="tpu_custom_call" | custom-call | tf_op jit(solution)/shard_map/cond/branch_1_fun/pallas_call | solution.py:112
  (13 shorter events, 0.1 us)
Async XLA Ops:
  20.0 20.6 %all-to-all-start = ((bf16[8,32,2048]{2,1,0:T(8,128)(2,1)}), bf16[8,32,2048]{2,1,0:T(8,128)(2,1)S(1)}, u32[]{:S(2)}, u32[]{:S(2)}) async-start(bf16[8,32,2048]{2,1,0:T(8,128)(2,1)} %branch_1_fun.3), calls=%async_computation | async-start | bytes 2097152 | tf_op jit(solution)/shard_map/cond/branch_1_fun/all_to_all | solution.py:162
  25.2 131.8 %all-gather.8.cloned.1.call-start = ((), (), s32[]{:S(2)}) async-start(), calls=%async_computation.4 | async-start | bytes 17301504 | tf_op jit(solution)/shard_map/cond/branch_1_fun/all_gather | solution.py:166
  157.0 5.8 %copy-start = (bf16[32,128,2048]{2,1,0:T(8,128)(2,1)S(1)}, bf16[32,128,2048]{2,1,0:T(8,128)(2,1)}, u32[]{:S(2)}) copy-start(bf16[32,128,2048]{2,1,0:T(8,128)(2,1)} %all-gather.8.cloned.1.call-done.packed_ref) | copy-start | bytes 50331652 | tf_op jit(solution)/shard_map/cond
Sparse Core Ops, SparseCore 0:
  42.7 114.2 all-gather.7

commit v2 on v1

--- a/solution.py
+++ b/solution.py
@@ -128,6 +128,197 @@
     )(irrep_blk, slot, amp, packed, residual)
 
 
+def spread_kernel(
+    irrep_ref, slot_ref, amp_ref, mine_ref, res_ref, out_ref, amps, held, sent, got, got_b, *, per_step
+):
+    n_row, n_col = 8, 4
+    row, z = lax.axis_index("row"), lax.axis_index("col")
+    rows = amps.shape[2]
+    half = round_up(rows // 2, 16)
+    top, bottom = pl.ds(0, half), pl.ds(half, rows - half)
+    core, x, y = row % 2, (row // 2) % 2, row // 4
+    sib = row + 1 - 2 * core
+    xn = row + 2 - 4 * x
+    yn = row + 4 - 8 * y
+    dg = xn + 4 - 8 * y
+    far = z // 2
+    middle = z + far * (3 - 2 * z)
+    order = [middle, 1 - middle, 2, 3]
+    order = [o + far * (3 - 2 * o) for o in order]
+    inner = z + 1 - 2 * far
+    outer = z - 1 + 2 * far
+
+    def place(r, c):
+        return {"row": r, "col": c}
+
+    def send(kind, j, r, to, part=None, recv=got):
+        slot = r * n_col + order[j]
+        ref = held.at[slot] if part is None else held.at[slot, part]
+        return pltpu.make_async_remote_copy(
+            src_ref=ref,
+            dst_ref=ref,
+            send_sem=sent.at[kind, j],
+            recv_sem=recv.at[slot],
+            device_id=to,
+            device_id_type=pl.DeviceIdType.MESH,
+        )
+
+    def await_chunk(j, r, part=None, recv=got):
+        send(0, j, r, place(sib, z), part, recv).wait_recv()
+
+    def compute(j, r_first, r_other):
+        def body(i, carry):
+            r = r_first + i * (r_other - r_first)
+            chunk = order[j] * n_row + r
+            slot = r * n_col + order[j]
+            for t in range(per_step):
+                g = irrep_ref[chunk * per_step + t]
+                cols = pl.ds(pl.multiple_of((chunk * per_step + t) * GRAIN, GRAIN), GRAIN)
+                piece = held[slot, :, t * GRAIN:(t + 1) * GRAIN]
+                ladder = jnp.dot(amps[g], piece, preferred_element_type=jnp.float32)
+                ladder = ladder.astype(jnp.bfloat16).astype(jnp.float32)
+                total = res_ref[:, cols].astype(jnp.float32) + ladder
+                out_ref[:, cols] = total.astype(jnp.bfloat16)
+            return carry
+
+        lax.fori_loop(0, 2, body, 0)
+
+    def by_z(j):
+        if j == 0:
+            return [(send(0, 0, row, place(row, inner)), False), (send(1, 0, row, place(row, outer)), True)]
+        to = inner if j == 1 else outer
+        return [(send(0 if j == 1 else 1, j, row, place(row, to)), True)]
+
+    def guarded(only_middle, act):
+        if only_middle:
+            pl.when(middle == 1)(act)
+        else:
+            act()
+
+    in_plane = lambda j: [
+        send(2, j, row, place(xn, z)),
+        send(3, j, row, place(yn, z)),
+        send(4, j, row, place(sib, z)),
+    ]
+    from_x = lambda j: [
+        send(5, j, xn, place(yn, z), top),
+        send(7, j, xn, place(sib, z)),
+    ]
+    from_y = lambda j: [
+        send(6, j, yn, place(xn, z), bottom, got_b),
+        send(8, j, yn, place(sib, z)),
+    ]
+    from_dg = lambda j: [send(9, j, dg, place(sib, z))]
+
+    def own(j):
+        if j > 0:
+            await_chunk(j, row)
+        for copy, only_middle in by_z(j):
+            guarded(only_middle, copy.start)
+        for copy in in_plane(j):
+            copy.start()
+
+    def near(j):
+        await_chunk(j, xn)
+        for copy in from_x(j):
+            copy.start()
+        await_chunk(j, yn)
+        for copy in from_y(j):
+            copy.start()
+
+    def diagonal(j):
+        await_chunk(j, dg, top)
+        await_chunk(j, dg, bottom, got_b)
+        for copy in from_dg(j):
+            copy.start()
+
+    def of_core(r):
+        return r + 1 - 2 * core
+
+    def own_done(j):
+        await_chunk(j, sib)
+        compute(j, row, sib)
+
+    def near_done(j):
+        await_chunk(j, of_core(xn))
+        compute(j, xn, of_core(xn))
+        await_chunk(j, of_core(yn))
+        compute(j, yn, of_core(yn))
+
+    def diagonal_done(j):
+        await_chunk(j, of_core(dg))
+        compute(j, dg, of_core(dg))
+
+    barrier = pltpu.get_barrier_semaphore()
+
+    def greet(to):
+        pl.semaphore_signal(barrier, inc=1, device_id=to, device_id_type=pl.DeviceIdType.MESH)
+
+    for to in (place(sib, z), place(xn, z), place(yn, z), place(row, inner)):
+        greet(to)
+    pl.when(middle == 1)(lambda: greet(place(row, outer)))
+    held[row * n_col + z] = mine_ref[0]
+    pl.semaphore_wait(barrier, 4 + middle)
+
+    own(0)
+    for g in range(NIRREP):
+        pick = one_hot_rows(slot_ref, g, rows)
+        amps[g] = lax.dot_general(
+            amp_ref[...], pick, (((1,), (1,)), ((), ())), preferred_element_type=jnp.float32
+        ).astype(jnp.bfloat16)
+    own_done(0)
+    own(1)
+    near(0)
+    own_done(1)
+    near_done(0)
+    own(2)
+    near(1)
+    diagonal(0)
+    own_done(2)
+    near_done(1)
+    diagonal_done(0)
+    own(3)
+    near(2)
+    diagonal(1)
+    own_done(3)
+    near_done(2)
+    diagonal_done(1)
+    near(3)
+    diagonal(2)
+    near_done(3)
+    diagonal_done(2)
+    diagonal(3)
+    diagonal_done(3)
+
+    for j in range(n_col):
+        for copy, only_middle in by_z(j):
+            guarded(only_middle, copy.wait_send)
+        for copy in in_plane(j) + from_x(j) + from_y(j) + from_dg(j):
+            copy.wait_send()
+
+
+def spread_add(amp, slot, irrep_blk, mine, residual, n_row, n_col):
+    _, rows, width = mine.shape
+    parts = n_row * n_col
+    vmem = pl.BlockSpec(memory_space=pltpu.VMEM)
+    return pl.pallas_call(
+        functools.partial(spread_kernel, per_step=width // GRAIN),
+        out_shape=jax.ShapeDtypeStruct(residual.shape, jnp.bfloat16),
+        in_specs=[pl.BlockSpec(memory_space=pltpu.SMEM), vmem, vmem, vmem, vmem],
+        out_specs=vmem,
+        scratch_shapes=[
+            pltpu.VMEM((NIRREP, amp.shape[0], rows), jnp.bfloat16),
+            pltpu.VMEM((parts, rows, width), jnp.bfloat16),
+            pltpu.SemaphoreType.DMA((10, n_col)),
+            pltpu.SemaphoreType.DMA((parts,)),
+            pltpu.SemaphoreType.DMA((parts,)),
+        ],
+        compiler_params=pltpu.CompilerParams(
+            vmem_limit_bytes=48 * MIB, collective_id=0, has_side_effects=True
+        ),
+    )(irrep_blk, slot, amp, mine, residual)
+
+
 def per_device(n_row, n_col, amplitudes, integrals, pair_irrep, block_offset, residual):
     steps, local_k, ab_local = integrals.shape
     n1 = steps * local_k
@@ -163,8 +354,10 @@
         ours = ours.reshape(n_row * cap1, ab_local // n_row)
         first = col * per_col + row * (per_col // n_row)
         mine2 = pack(ours, slot2, irrep_blk, first, cap2, 1)
+        amp = amplitudes.reshape(amplitudes.shape[0], -1)
+        if (n_row, n_col) == (8, 4):
+            return spread_add(amp, slot3, irrep_blk, mine2, residual, n_row, n_col)
         packed = lax.all_gather(mine2, ("row", "col"), axis=0, tiled=True)
-        amp = amplitudes.reshape(amplitudes.shape[0], -1)
         return ladder_add(amp, slot3, irrep_blk, packed, residual, n_row, n_col)
 
     def full(amplitudes, integrals, residual):

time: 194 us -> 135 us (0.70)
  waiting for transfers between devices: 128 us -> 13.9 us
  Pallas kernels: 32.1 us -> 88.2 us
    all_gather x1 -> x0, waiting for transfers between devices: 114 us -> none  [sparse(): packed = lax.all_gather(mine2, ('row', 'col'), axis=0, tiled=True)]
    pallas_call x1, Pallas kernels: 23.2 us -> 80.1 us  [spread_add(): pl.pallas_call(functools.partial(spread_kernel, per_step=width // GRAIN),...]
    cond x2 -> x0, local copies, waits for them, and re-layouts: 5.77 us -> none
    unnamed x0 -> x1, local copies, waits for them, and re-layouts: none -> 5.18 us
  transfers between devices with their start and end apart: 2 -> 1, of which waited for: 2 -> 1; matrix products, arithmetic and copies ran while one was open for 1% -> 1% of each run, Pallas kernels for 0% -> 0%
where the time goes in v2:
time: 135 us; the launch traced here: 134 us
  Pallas kernels  88.2 us (65%)
  between operations  14.8 us (11%)
  waiting for transfers between devices  13.9 us (10%)
  local copies, waits for them, and re-layouts  8.47 us (6%)
  starting transfers between devices  5.17 us (4%)
  other arithmetic  3.25 us (2%)
    pallas_call x1, Pallas kernels, spread_add(): pl.pallas_call(functools.partial(spread_kernel, per_step=width // GRAIN),...  80.1 us
    all_to_all x1, waiting for transfers between devices, sparse(): ours = lax.all_to_all(mine1, 'row', split_axis=0, concat_axis=0, tiled=True)  13.9 us
    pallas_call x2, Pallas kernels, pack(): pl.pallas_call(functools.partial(pack_kernel, blocks=blocks, per_step=wid...  8.15 us
    unnamed x1, local copies, waits for them, and re-layouts  5.18 us
    all_to_all x1, starting transfers between devices, sparse(): ours = lax.all_to_all(mine1, 'row', split_axis=0, concat_axis=0, tiled=True)  5.17 us
  transfers between devices with their start and end apart: 1, of which 1 were waited for; matrix products, arithmetic and copies ran while one was open for 1% of the time, Pallas kernels for 0%

profile of v2, /device:TPU:0, one launch (start us, length us, event | category | flops | bytes accessed | tf_op | source)
XLA Modules:
  0.0 134.0 jit_solution(15203174679105619583)
XLA Ops:
  6.5 0.7 slice.37
  7.3 0.8 reshape.50
  8.0 0.1 eq.63
  8.1 0.1 compare_convert_fusion
  8.2 2.0 %reduce_window_sum.22 = s32[8,8,96]{2,1,0:T(8,128)S(1)} reduce-window(s32[8,8,96]{2,1,0:T(8,128)S(1)} %copy.50, s32[]{:T(128)} %constant.44.clone.1), window={size=1x1x96 pad=0_0x0_0x95_0}, to_apply=%region_0.0 | reduce-window | flops 583680 | bytes 49156 | tf_op jit(solution)/shard_map/jit(cumsum)/reduce_window_sum | solution.py:332
  10.2 0.1 slice.44
  10.4 0.9 subtract_reduce_fusion
  12.6 0.1 sub.14
  12.8 0.1 select_bitcast_fusion
  12.9 109.1 %conditional.1 = (bf16[40,65536]{1,0:T(8,128)(2,1)}) conditional(s32[]{:T(128)} %convert_element_type.34, (bf16[40,65536]{1,0:T(8,128)(2,1)}, s32[3,256]{1,0:T(4,128)}, s32[9]{0:T(128)}, bf16[3,32,16384]{2,1,0:T(8,128)(2,1)}, bf16[40,3,256]{2,0,1:T(8,128)(2,1)}) %tuple.15, (s32[512,7]{0,1:T(8,128)S(1)}, s32[8,3,8,32]{3,1,2,0:T(4,128)S(1)}, ...), branch_computations={%region_4.6_spmd, %region_6.8_spmd} | conditional | flops 4070391808 | bytes 227321024 | solution.py:366
  13.2 7.0 %branch_1_fun.3 = bf16[8,32,2048]{2,1,0:T(8,128)(2,1)} custom-call(s32[513]{0:T(1024)S(1)} %get-tuple-element.170.irrep_ref, s32[8,96]{1,0:T(8,128)S(1)} %fusion.18.slot_ref, bf16[3,32,16384]{2,1,0:T(8,128)(2,1)} %get-tuple-element.91.x_ref), custom_call_target="tpu_custom_call" | custom-call | tf_op jit(solution)/shard_map/cond/branch_1_fun/pallas_call | solution.py:72
  20.2 5.2 %all-to-all-start = ((bf16[8,32,2048]{2,1,0:T(8,128)(2,1)}), bf16[8,32,2048]{2,1,0:T(8,128)(2,1)S(1)}, u32[]{:S(2)}, u32[]{:S(2)}) async-start(bf16[8,32,2048]{2,1,0:T(8,128)(2,1)} %branch_1_fun.3), calls=%async_computation | async-start | bytes 2097152 | tf_op jit(solution)/shard_map/cond/branch_1_fun/all_to_all | solution.py:353
  25.3 0.1 lt.30
  25.4 0.1 lt.24
  25.5 0.1 copy.54
  25.6 0.1 lt.27
  25.7 0.1 lt.28
  25.8 0.1 add.52
  25.8 0.1 add.53
  25.9 0.8 copy.59
  26.8 0.1 reshape.46.slot_ref
  26.9 13.9 %all-to-all-done = bf16[8,32,2048]{2,1,0:T(8,128)(2,1)S(1)} async-done(((bf16[8,32,2048]{2,1,0:T(8,128)(2,1)}), bf16[8,32,2048]{2,1,0:T(8,128)(2,1)S(1)}, u32[]{:S(2)}, u32[]{:S(2)}) %all-to-all-start) | async-done | bytes 1048608 | tf_op jit(solution)/shard_map/cond/branch_1_fun/all_to_all | solution.py:353
  40.8 1.2 branch_1_fun.4.mine_ref
  41.9 80.1 %branch_1_fun.5 = bf16[40,65536]{1,0:T(8,128)(2,1)} custom-call(s32[512]{0:T(512)S(1)} %reduce_sum.18.irrep_ref, s32[8,768]{1,0:T(8,128)S(1)} %reshape.46.slot_ref, bf16[40,768]{1,0:T(8,128)(2,1)S(1)} %bitcast.60, bf16[1,128,2048]{2,1,0:T(8,128)(2,1)S(1)} %branch_1_fun.4.mine_ref, bf16[40,65536]{1,0:T(8,128)(2,1)} %get-tuple-element.92.res_ref), custom_call_target="tpu_custom_call" | custom-call | tf_op jit(solution)/shard_map/cond/branch_1_fun/pallas_call | solution.py:304
  122.0 5.2 %copy.65 = bf16[40,65536]{1,0:T(8,128)(2,1)} copy(bf16[40,65536]{1,0:T(8,128)(2,1)} %get-tuple-element.93) | data formatting | bytes 10485760
  (13 shorter events, 0.1 us)
Async XLA Ops:
  20.2 20.6 %all-to-all-start = ((bf16[8,32,2048]{2,1,0:T(8,128)(2,1)}), bf16[8,32,2048]{2,1,0:T(8,128)(2,1)S(1)}, u32[]{:S(2)}, u32[]{:S(2)}) async-start(bf16[8,32,2048]{2,1,0:T(8,128)(2,1)} %branch_1_fun.3), calls=%async_computation | async-start | bytes 2097152 | tf_op jit(solution)/shard_map/cond/branch_1_fun/all_to_all | solution.py:353

commit v3 on v2

--- a/solution.py
+++ b/solution.py
@@ -129,13 +129,21 @@
 
 
 def spread_kernel(
-    irrep_ref, slot_ref, amp_ref, mine_ref, res_ref, out_ref, amps, held, sent, got, got_b, *, per_step
+    irrep_ref, slot_ref, amp_ref, mine_ref, res_ref, out_ref, amps, held, sent, got, got_b, got_c, *, per_step
 ):
     n_row, n_col = 8, 4
     row, z = lax.axis_index("row"), lax.axis_index("col")
     rows = amps.shape[2]
     half = round_up(rows // 2, 16)
-    top, bottom = pl.ds(0, half), pl.ds(half, rows - half)
+    along_rows = rows - 32
+    along_part = pl.ds(0, along_rows)
+
+    def top(j):
+        return pl.ds(0, half) if j == 0 else pl.ds(along_rows, 16)
+
+    def bottom(j):
+        return pl.ds(half, rows - half) if j == 0 else pl.ds(along_rows + 16, 16)
+
     core, x, y = row % 2, (row // 2) % 2, row // 4
     sib = row + 1 - 2 * core
     xn = row + 2 - 4 * x
@@ -183,11 +191,17 @@
 
         lax.fori_loop(0, 2, body, 0)
 
-    def by_z(j):
+    def by_z(j, r=row, part=None, recv=got, kind=0):
         if j == 0:
-            return [(send(0, 0, row, place(row, inner)), False), (send(1, 0, row, place(row, outer)), True)]
+            return [
+                (send(kind, 0, r, place(row, inner), part, recv), False),
+                (send(kind + 1, 0, r, place(row, outer), part, recv), True),
+            ]
         to = inner if j == 1 else outer
-        return [(send(0 if j == 1 else 1, j, row, place(row, to)), True)]
+        return [(send(kind if j == 1 else kind + 1, j, r, place(row, to), part, recv), True)]
+
+    def dg_by_z(j):
+        return by_z(j, dg, along_part, got_c, 10)
 
     def guarded(only_middle, act):
         if only_middle:
@@ -201,11 +215,11 @@
         send(4, j, row, place(sib, z)),
     ]
     from_x = lambda j: [
-        send(5, j, xn, place(yn, z), top),
+        send(5, j, xn, place(yn, z), top(j)),
         send(7, j, xn, place(sib, z)),
     ]
     from_y = lambda j: [
-        send(6, j, yn, place(xn, z), bottom, got_b),
+        send(6, j, yn, place(xn, z), bottom(j), got_b),
         send(8, j, yn, place(sib, z)),
     ]
     from_dg = lambda j: [send(9, j, dg, place(sib, z))]
@@ -226,9 +240,17 @@
         for copy in from_y(j):
             copy.start()
 
+    def along(j):
+        await_chunk(j, dg, along_part, got_c)
+        for copy, only_middle in dg_by_z(j):
+            guarded(only_middle, copy.start)
+
     def diagonal(j):
-        await_chunk(j, dg, top)
-        await_chunk(j, dg, bottom, got_b)
+        await_chunk(j, dg, top(j))
+        await_chunk(j, dg, bottom(j), got_b)
+        if j == 0:
+            for copy, only_middle in dg_by_z(0):
+                guarded(only_middle, copy.start)
         for copy in from_dg(j):
             copy.start()
 
@@ -270,28 +292,31 @@
     own(1)
     near(0)
     own_done(1)
-    near_done(0)
     own(2)
     near(1)
+    near_done(0)
     diagonal(0)
+    own(3)
     own_done(2)
     near_done(1)
+    along(1)
+    near(2)
     diagonal_done(0)
-    own(3)
-    near(2)
+    own_done(3)
+    along(2)
     diagonal(1)
-    own_done(3)
     near_done(2)
+    near(3)
+    along(3)
+    diagonal(2)
     diagonal_done(1)
-    near(3)
-    diagonal(2)
+    diagonal(3)
     near_done(3)
     diagonal_done(2)
-    diagonal(3)
     diagonal_done(3)
 
     for j in range(n_col):
-        for copy, only_middle in by_z(j):
+        for copy, only_middle in by_z(j) + dg_by_z(j):
             guarded(only_middle, copy.wait_send)
         for copy in in_plane(j) + from_x(j) + from_y(j) + from_dg(j):
             copy.wait_send()
@@ -309,7 +334,8 @@
         scratch_shapes=[
             pltpu.VMEM((NIRREP, amp.shape[0], rows), jnp.bfloat16),
             pltpu.VMEM((parts, rows, width), jnp.bfloat16),
-            pltpu.SemaphoreType.DMA((10, n_col)),
+            pltpu.SemaphoreType.DMA((12, n_col)),
+            pltpu.SemaphoreType.DMA((parts,)),
             pltpu.SemaphoreType.DMA((parts,)),
             pltpu.SemaphoreType.DMA((parts,)),
         ],
@@ -319,11 +345,116 @@
     )(irrep_blk, slot, amp, mine, residual)
 
 
+def exchange_kernel(
+    irrep_ref, slot1_ref, slot2_ref, x_ref, out_ref,
+    x, mine, ours, pick1, pick2, loaded, sent, got, *, n_row, per_step
+):
+    row, col = lax.axis_index("row"), lax.axis_index("col")
+    width = per_step * GRAIN
+    cap1, cap2 = pick1.shape[1], pick2.shape[1]
+    turns = list(range(1, n_row)) + [0]
+
+    def peer(k):
+        return (row + k) % n_row
+
+    def load(k):
+        cols = pl.ds(pl.multiple_of(peer(k) * width, width), width)
+        return pltpu.make_async_copy(x_ref.at[:, :, cols], x.at[k], loaded.at[k])
+
+    def send(k):
+        return pltpu.make_async_remote_copy(
+            src_ref=mine.at[k],
+            dst_ref=ours.at[row],
+            send_sem=sent.at[k],
+            recv_sem=got.at[row],
+            device_id={"row": peer(k), "col": col},
+            device_id_type=pl.DeviceIdType.MESH,
+        )
+
+    for k in turns:
+        load(k).start()
+    barrier = pltpu.get_barrier_semaphore()
+    for k in turns[:-1]:
+        pl.semaphore_signal(
+            barrier, inc=1, device_id={"row": peer(k), "col": col},
+            device_id_type=pl.DeviceIdType.MESH,
+        )
+    for g in range(NIRREP):
+        pick1[g] = one_hot_rows(slot1_ref, g, cap1)
+
+    def pack_into(put, picks, rows, block, first):
+        for t in range(0, per_step, 2):
+            two = jnp.concatenate([picks[irrep_ref[first + t]], picks[irrep_ref[first + t + 1]]], axis=0)
+            both = jnp.dot(
+                two, block[:, t * GRAIN:(t + 2) * GRAIN], preferred_element_type=jnp.float32
+            ).astype(jnp.bfloat16)
+            put(t, both[:rows, :GRAIN])
+            put(t + 1, both[rows:, GRAIN:])
+
+    for k in turns:
+        load(k).wait()
+        block = x[k].reshape(-1, width)
+        first = (col * n_row + peer(k)) * per_step
+
+        def put(t, piece):
+            cols = slice(t * GRAIN, (t + 1) * GRAIN)
+            if k > 0:
+                mine[k, :, cols] = piece
+            else:
+                ours[row, :, cols] = piece
+
+        pack_into(put, pick1, cap1, block, first)
+        if k == turns[0]:
+            pl.semaphore_wait(barrier, n_row - 1)
+        if k > 0:
+            send(k).start()
+
+    for g in range(NIRREP):
+        pick2[g] = one_hot_rows(slot2_ref, g, cap2)
+    for k in turns[:-1]:
+        source = (row + n_row - k) % n_row
+        pltpu.make_async_copy(mine.at[k], ours.at[source], got.at[source]).wait()
+
+    def put_out(t, piece):
+        out_ref[0, :, t * GRAIN:(t + 1) * GRAIN] = piece
+
+    block = ours[...].reshape(n_row * cap1, width)
+    pack_into(put_out, pick2, cap2, block, (col * n_row + row) * per_step)
+    for k in turns[:-1]:
+        send(k).wait_send()
+
+
+def exchange(integrals, slot1, slot2, irrep_blk, cap1, cap2, n_row):
+    steps, local_k, ab_local = integrals.shape
+    width = ab_local // n_row
+    vmem = pl.BlockSpec(memory_space=pltpu.VMEM)
+    return pl.pallas_call(
+        functools.partial(exchange_kernel, n_row=n_row, per_step=width // GRAIN),
+        out_shape=jax.ShapeDtypeStruct((1, cap2, width), jnp.bfloat16),
+        in_specs=[pl.BlockSpec(memory_space=pltpu.SMEM), vmem, vmem, pl.BlockSpec(memory_space=pl.ANY)],
+        out_specs=vmem,
+        scratch_shapes=[
+            pltpu.VMEM((n_row, steps, local_k, width), jnp.bfloat16),
+            pltpu.VMEM((n_row, cap1, width), jnp.bfloat16),
+            pltpu.VMEM((n_row, cap1, width), jnp.bfloat16),
+            pltpu.VMEM((NIRREP, cap1, steps * local_k), jnp.bfloat16),
+            pltpu.VMEM((NIRREP, cap2, n_row * cap1), jnp.bfloat16),
+            pltpu.SemaphoreType.DMA((n_row,)),
+            pltpu.SemaphoreType.DMA((n_row,)),
+            pltpu.SemaphoreType.DMA((n_row,)),
+        ],
+        compiler_params=pltpu.CompilerParams(
+            vmem_limit_bytes=24 * MIB, collective_id=1, has_side_effects=True
+        ),
+    )(irrep_blk, slot1, slot2, integrals)
+
+
 def per_device(n_row, n_col, amplitudes, integrals, pair_irrep, block_offset, residual):
     steps, local_k, ab_local = integrals.shape
     n1 = steps * local_k
     cap1 = round_up(-(-n1 // 3), 16)
     cap2 = round_up(-(-n1 * n_row // 6), 16)
+    tight = cap2 - 16
     row, col = lax.axis_index("row"), lax.axis_index("col")
 
     labels = pair_irrep.reshape(steps, n_row, local_k).transpose(1, 0, 2).reshape(n_row, n1)
@@ -334,7 +465,10 @@
     rank = jnp.where(mine, running - 1, -1)
     upto = jnp.cumsum(count, axis=1)
     base = upto - count
-    fits = (jnp.max(count) <= cap1) & (jnp.max(upto) <= cap2)
+    most = jnp.max(upto)
+    level = jnp.where(
+        jnp.max(count) > cap1, 2, (most > tight).astype(jnp.int32) + (most > cap2).astype(jnp.int32)
+    )
 
     slot1 = lax.dynamic_index_in_dim(rank, row, axis=1, keepdims=False)
     spot = lax.iota(jnp.int32, cap1)
@@ -347,23 +481,28 @@
     starts = lax.iota(jnp.int32, blocks) * GRAIN
     irrep_blk = jnp.sum((starts[:, None] >= block_offset[None, 1:-1]).astype(jnp.int32), axis=1)
 
+    per_col = ab_local // GRAIN
+
+    def by_links(amplitudes, integrals, residual):
+        mine = exchange(integrals, slot1, slot2, irrep_blk, cap1, tight, n_row)
+        amp = amplitudes.reshape(amplitudes.shape[0], -1)
+        return spread_add(amp, slot3, irrep_blk, mine, residual, n_row, n_col)
+
     def sparse(amplitudes, integrals, residual):
-        per_col = ab_local // GRAIN
         mine1 = pack(integrals, slot1, irrep_blk, col * per_col, cap1, n_row)
         ours = lax.all_to_all(mine1, "row", split_axis=0, concat_axis=0, tiled=True)
         ours = ours.reshape(n_row * cap1, ab_local // n_row)
         first = col * per_col + row * (per_col // n_row)
         mine2 = pack(ours, slot2, irrep_blk, first, cap2, 1)
+        packed = lax.all_gather(mine2, ("row", "col"), axis=0, tiled=True)
         amp = amplitudes.reshape(amplitudes.shape[0], -1)
-        if (n_row, n_col) == (8, 4):
-            return spread_add(amp, slot3, irrep_blk, mine2, residual, n_row, n_col)
-        packed = lax.all_gather(mine2, ("row", "col"), axis=0, tiled=True)
         return ladder_add(amp, slot3, irrep_blk, packed, residual, n_row, n_col)
 
     def full(amplitudes, integrals, residual):
         return dense(amplitudes, integrals, pair_irrep, block_offset, residual)
 
-    return lax.cond(fits, sparse, full, amplitudes, integrals, residual)
+    quick = by_links if (n_row, n_col) == (8, 4) else sparse
+    return lax.switch(level, [quick, sparse, full], amplitudes, integrals, residual)
 
 
 def solution(mesh):

time: 135 us -> 119 us (0.88)
  waiting for transfers between devices: 13.9 us -> 0 us
  starting transfers between devices: 5.17 us -> 0 us
  Pallas kernels: 88.2 us -> 91.4 us
    all_to_all x1 -> x0, waiting for transfers between devices: 13.9 us -> none  [sparse(): ours = lax.all_to_all(mine1, 'row', split_axis=0, concat_axis=0, tiled=True)]
    pallas_call x2 -> x1, Pallas kernels: 8.15 us -> 16.5 us  [exchange(): pl.pallas_call(functools.partial(exchange_kernel, n_row=n_row, per_step=w...]
    pallas_call x1, Pallas kernels: 80.1 us -> 74.8 us  [spread_add(): pl.pallas_call(functools.partial(spread_kernel, per_step=width // GRAIN),...]
    all_to_all x1 -> x0, starting transfers between devices: 5.17 us -> none  [sparse(): ours = lax.all_to_all(mine1, 'row', split_axis=0, concat_axis=0, tiled=True)]
  transfers between devices with their start and end apart: 1 -> 0, of which waited for: 1 -> 0; matrix products, arithmetic and copies ran while one was open for 1% -> 0% of each run, Pallas kernels for 0% -> 0%
where the time goes in v3:
time: 119 us
  Pallas kernels  91.4 us (77%)
  between operations  15.5 us (13%)
  local copies, waits for them, and re-layouts  8.26 us (7%)
  other arithmetic  3.38 us (3%)
    pallas_call x1, Pallas kernels, spread_add(): pl.pallas_call(functools.partial(spread_kernel, per_step=width // GRAIN),...  74.8 us
    pallas_call x1, Pallas kernels, exchange(): pl.pallas_call(functools.partial(exchange_kernel, n_row=n_row, per_step=w...  16.5 us
    unnamed x1, local copies, waits for them, and re-layouts  5.18 us

profile of v3, /device:TPU:0, one launch (start us, length us, event | category | flops | bytes accessed | tf_op | source)
XLA Modules:
  0.0 118.7 jit_solution(10724754035671585454)
XLA Ops:
  6.5 0.7 slice.37
  7.3 0.1 convert_reduce_fusion.1
  7.4 0.1 lt.34
  7.4 0.8 reshape.49
  8.2 0.1 eq.63
  8.3 2.0 %reduce_window_sum.22 = s32[8,8,96]{2,1,0:T(8,128)S(1)} reduce-window(s32[8,8,96]{2,1,0:T(8,128)S(1)} %get-tuple-element.181, s32[]{:T(128)} %constant.17.clone.1), window={size=1x1x96 pad=0_0x0_0x95_0}, to_apply=%region_0.0 | reduce-window | flops 583680 | bytes 49156 | tf_op jit(solution)/shard_map/jit(cumsum)/reduce_window_sum | solution.py:463
  10.3 0.1 slice.44
  10.5 1.1 slice_reduce_fusion
  13.6 0.1 lt.37
  13.6 0.1 lt.38
  13.7 0.1 add.62
  13.8 0.1 add.63
  13.9 0.1 sub.12
  14.0 0.1 select_bitcast_fusion
  14.2 0.1 reshape.50
  14.2 92.4 %conditional.1 = (bf16[40,65536]{1,0:T(8,128)(2,1)}) conditional(s32[]{:T(128)} %clamp.3, (bf16[40,3,256]{2,0,1:T(8,128)(2,1)}, s32[512]{0:T(512)S(1)}, s32[8,96]{1,0:T(8,128)S(1)}, s32[8,256]{1,0:T(8,128)S(1)}, bf16[3,32,16384]{2,1,0:T(8,128)(2,1)}, /*index=5*/s32[8,768]{1,0:T(8,128)S(1)}, bf16[40,65536]{1,0:T(8,128)(2,1)}) %tuple.49, ...), branch_computations={%region_5.6_spmd, %region_6.7_spmd, %region_7.9_spmd} | conditional | flops 4070391808 | bytes 227321024 | solution.py:505
  14.2 0.8 copy.57
  15.1 16.5 %branch_0_fun.2.mine_ref = bf16[1,112,2048]{2,1,0:T(8,128)(2,1)S(1)} custom-call(s32[512]{0:T(512)S(1)} %get-tuple-element.50.irrep_ref, s32[8,96]{1,0:T(8,128)S(1)} %get-tuple-element.54.slot1_ref, s32[8,256]{1,0:T(8,128)S(1)} %get-tuple-element.55.slot2_ref, bf16[3,32,16384]{2,1,0:T(8,128)(2,1)} %get-tuple-element.56.x_ref), custom_call_target="tpu_custom_call" | custom-call | tf_op jit(solution)/shard_map/cond/branch_0_fun/pallas_call | solution.py:431
  31.6 74.8 %branch_0_fun.3 = bf16[40,65536]{1,0:T(8,128)(2,1)} custom-call(s32[512]{0:T(512)S(1)} %get-tuple-element.50.irrep_ref, s32[8,768]{1,0:T(8,128)S(1)} %get-tuple-element.52.slot_ref, bf16[40,768]{1,0:T(8,128)(2,1)S(1)} %bitcast.61, bf16[1,112,2048]{2,1,0:T(8,128)(2,1)S(1)} %branch_0_fun.2.mine_ref, bf16[40,65536]{1,0:T(8,128)(2,1)} %get-tuple-element.57.res_ref), custom_call_target="tpu_custom_call" | custom-call | tf_op jit(solution)/shard_map/cond/branch_0_fun/pallas_call | solution.py:329
  106.7 5.2 %copy.66 = bf16[40,65536]{1,0:T(8,128)(2,1)} copy(bf16[40,65536]{1,0:T(8,128)(2,1)} %get-tuple-element.72) | data formatting | bytes 10485760
  (9 shorter events, 0.1 us)

commit v4 on v3

--- a/solution.py
+++ b/solution.py
@@ -2,6 +2,7 @@
 
 import jax
 import jax.numpy as jnp
+import numpy as np
 from jax import lax
 from jax.experimental import pallas as pl
 from jax.experimental.pallas import tpu as pltpu
@@ -129,7 +130,8 @@
 
 
 def spread_kernel(
-    irrep_ref, slot_ref, amp_ref, mine_ref, res_ref, out_ref, amps, held, sent, got, got_b, got_c, *, per_step
+    irrep_ref, slot_ref, amp_ref, mine_ref, res_hbm, out_hbm,
+    amps, held, res_ref, out_ref, sent, got, got_b, got_c, read, wrote, *, per_step
 ):
     n_row, n_col = 8, 4
     row, z = lax.axis_index("row"), lax.axis_index("col")
@@ -173,6 +175,11 @@
 
     def await_chunk(j, r, part=None, recv=got):
         send(0, j, r, place(sib, z), part, recv).wait_recv()
+
+    def write(r, c):
+        width = per_step * GRAIN
+        cols = pl.ds(pl.multiple_of((c * n_row + r) * width, width), width)
+        return pltpu.make_async_copy(out_ref.at[:, cols], out_hbm.at[:, cols], wrote.at[r * n_col + c])
 
     def compute(j, r_first, r_other):
         def body(i, carry):
@@ -187,6 +194,7 @@
                 ladder = ladder.astype(jnp.bfloat16).astype(jnp.float32)
                 total = res_ref[:, cols].astype(jnp.float32) + ladder
                 out_ref[:, cols] = total.astype(jnp.bfloat16)
+            write(r, order[j]).start()
             return carry
 
         lax.fori_loop(0, 2, body, 0)
@@ -271,6 +279,8 @@
         await_chunk(j, of_core(dg))
         compute(j, dg, of_core(dg))
 
+    reading = pltpu.make_async_copy(res_hbm, res_ref, read)
+    reading.start()
     barrier = pltpu.get_barrier_semaphore()
 
     def greet(to):
@@ -288,6 +298,7 @@
         amps[g] = lax.dot_general(
             amp_ref[...], pick, (((1,), (1,)), ((), ())), preferred_element_type=jnp.float32
         ).astype(jnp.bfloat16)
+    reading.wait()
     own_done(0)
     own(1)
     near(0)
@@ -316,6 +327,8 @@
     diagonal_done(3)
 
     for j in range(n_col):
+        for r in range(n_row):
+            write(r, j).wait()
         for copy, only_middle in by_z(j) + dg_by_z(j):
             guarded(only_middle, copy.wait_send)
         for copy in in_plane(j) + from_x(j) + from_y(j) + from_dg(j):
@@ -326,17 +339,22 @@
     _, rows, width = mine.shape
     parts = n_row * n_col
     vmem = pl.BlockSpec(memory_space=pltpu.VMEM)
+    hbm = pl.BlockSpec(memory_space=pl.ANY)
     return pl.pallas_call(
         functools.partial(spread_kernel, per_step=width // GRAIN),
         out_shape=jax.ShapeDtypeStruct(residual.shape, jnp.bfloat16),
-        in_specs=[pl.BlockSpec(memory_space=pltpu.SMEM), vmem, vmem, vmem, vmem],
-        out_specs=vmem,
+        in_specs=[pl.BlockSpec(memory_space=pltpu.SMEM), vmem, vmem, vmem, hbm],
+        out_specs=hbm,
         scratch_shapes=[
             pltpu.VMEM((NIRREP, amp.shape[0], rows), jnp.bfloat16),
             pltpu.VMEM((parts, rows, width), jnp.bfloat16),
+            pltpu.VMEM(residual.shape, jnp.bfloat16),
+            pltpu.VMEM(residual.shape, jnp.bfloat16),
             pltpu.SemaphoreType.DMA((12, n_col)),
             pltpu.SemaphoreType.DMA((parts,)),
             pltpu.SemaphoreType.DMA((parts,)),
+            pltpu.SemaphoreType.DMA((parts,)),
+            pltpu.SemaphoreType.DMA,
             pltpu.SemaphoreType.DMA((parts,)),
         ],
         compiler_params=pltpu.CompilerParams(
@@ -457,25 +475,35 @@
     tight = cap2 - 16
     row, col = lax.axis_index("row"), lax.axis_index("col")
 
-    labels = pair_irrep.reshape(steps, n_row, local_k).transpose(1, 0, 2).reshape(n_row, n1)
-    irreps = lax.iota(jnp.int32, NIRREP)
-    mine = labels[None] == irreps[:, None, None]
-    running = jnp.cumsum(mine.astype(jnp.int32), axis=2)
-    count = running[:, :, -1]
-    rank = jnp.where(mine, running - 1, -1)
-    upto = jnp.cumsum(count, axis=1)
-    base = upto - count
+    pairs = np.arange(steps * local_k * n_row)
+    holder = pairs // local_k % n_row
+    same = holder[:, None] == holder[None, :]
+    within = same & (pairs[:, None] <= pairs[None, :])
+    ahead = holder[:, None] < holder[None, :]
+    rows = np.arange(n_row)
+    held = holder[:, None] == rows[None, :]
+    before = holder[:, None] < rows[None, :]
+    tally = np.concatenate([within, within | ahead, held, before], axis=1)
+    mine = pair_irrep.reshape(1, -1) == lax.iota(jnp.int32, NIRREP)[:, None]
+    sums = jnp.dot(
+        mine.astype(jnp.bfloat16), jnp.asarray(tally, jnp.bfloat16),
+        preferred_element_type=jnp.float32,
+    ).astype(jnp.int32)
+    depth = pairs.size
+    rank = jnp.where(mine, sums[:, :depth] - 1, -1).reshape(NIRREP, steps, n_row, local_k)
+    slot3 = jnp.where(mine, sums[:, depth:2 * depth] - 1, -1)
+    count = sums[:, 2 * depth:2 * depth + n_row]
+    base = sums[:, 2 * depth + n_row:]
+    upto = base + count
     most = jnp.max(upto)
     level = jnp.where(
         jnp.max(count) > cap1, 2, (most > tight).astype(jnp.int32) + (most > cap2).astype(jnp.int32)
     )
 
-    slot1 = lax.dynamic_index_in_dim(rank, row, axis=1, keepdims=False)
+    slot1 = lax.dynamic_index_in_dim(rank, row, axis=2, keepdims=False).reshape(NIRREP, n1)
     spot = lax.iota(jnp.int32, cap1)
     slot2 = jnp.where(spot[None, None] < count[:, :, None], base[:, :, None] + spot, -1)
     slot2 = slot2.reshape(NIRREP, n_row * cap1)
-    slot3 = jnp.where(mine, base[:, :, None] + rank, -1)
-    slot3 = slot3.reshape(NIRREP, n_row, steps, local_k).transpose(0, 2, 1, 3).reshape(NIRREP, -1)
 
     blocks = n_col * ab_local // GRAIN
     starts = lax.iota(jnp.int32, blocks) * GRAIN

time: 119 us -> 115 us (0.966)
  Pallas kernels: 91.4 us -> 88 us
  other arithmetic: 3.38 us -> 0.84 us
  matrix products: 0 us -> 2.16 us
    pallas_call x1, Pallas kernels: 74.8 us -> 71.5 us  [spread_add(): pl.pallas_call(functools.partial(spread_kernel, per_step=width // GRAIN),...]
    dot_general x0 -> x1, matrix products: none -> 2.16 us  [per_device(): jnp.dot(mine.astype(jnp.bfloat16), jnp.asarray(tally, jnp.bfloat16), pref...]
    another operation x2 -> x0, other arithmetic: 2.06 us -> none  [the longest x1 2.02 us: per_device(): running = jnp.cumsum(mine.astype(jnp.int32), axis=2)]
where the time goes in v4:
time: 115 us
  Pallas kernels  88 us (77%)
  between operations  15.3 us (13%)
  local copies, waits for them, and re-layouts  8.04 us (7%)
  matrix products  2.16 us (2%)
    pallas_call x1, Pallas kernels, spread_add(): pl.pallas_call(functools.partial(spread_kernel, per_step=width // GRAIN),...  71.5 us
    pallas_call x1, Pallas kernels, exchange(): pl.pallas_call(functools.partial(exchange_kernel, n_row=n_row, per_step=w...  16.5 us
    unnamed x1, local copies, waits for them, and re-layouts  5.18 us

profile of v4, /device:TPU:0, one launch (start us, length us, event | category | flops | bytes accessed | tf_op | source)
XLA Modules:
  0.0 114.7 jit_solution(18183453751477098114)
XLA Ops:
  6.5 0.7 slice.47
  7.3 0.1 convert_reduce_fusion.1
  7.4 0.7 eq.56
  8.1 0.1 lt.32
  8.1 2.2 %convolution_convert_fusion = s32[8,1552]{1,0:T(8,128)S(1)} fusion(bf16[768,1552]{1,0:T(8,128)(2,1)} %constant.48.clone, s32[768]{0:T(1024)S(1)} %eq.56), kind=kOutput, calls=%fused_computation.31 | convolution fusion | flops 19089536 | bytes 2436608 | tf_op jit(solution)/shard_map/dot_general | solution.py:488
  10.3 0.7 add_reduce_fusion
  13.0 0.1 lt.34
  13.0 0.1 lt.35
  13.1 0.1 add.53
  13.2 0.1 add.54
  13.3 0.1 reshape.44
  13.4 0.1 dynamic-slice_reduce_fusion
  13.4 0.1 reshape.45
  13.5 89.1 %conditional.1 = (bf16[40,65536]{1,0:T(8,128)(2,1)}) conditional(s32[]{:T(128)} %clamp.3, (bf16[40,3,256]{2,0,1:T(8,128)(2,1)}, s32[512]{0:T(512)S(1)}, s32[8,96]{1,0:T(8,128)S(1)}, s32[8,256]{1,0:T(8,128)S(1)}, bf16[3,32,16384]{2,1,0:T(8,128)(2,1)}, /*index=5*/s32[8,768]{1,0:T(8,128)S(1)}, bf16[40,65536]{1,0:T(8,128)(2,1)}) %tuple.14, ...), branch_computations={%region_3.4_spmd, %region_4.5_spmd, %region_5.7_spmd} | conditional | flops 4070391808 | bytes 227321024 | solution.py:533
  13.5 0.8 copy.44
  14.4 16.5 %branch_0_fun.2.mine_ref = bf16[1,112,2048]{2,1,0:T(8,128)(2,1)S(1)} custom-call(s32[512]{0:T(512)S(1)} %get-tuple-element.50.irrep_ref, s32[8,96]{1,0:T(8,128)S(1)} %get-tuple-element.54.slot1_ref, s32[8,256]{1,0:T(8,128)S(1)} %get-tuple-element.55.slot2_ref, bf16[3,32,16384]{2,1,0:T(8,128)(2,1)} %get-tuple-element.56.x_ref), custom_call_target="tpu_custom_call" | custom-call | tf_op jit(solution)/shard_map/cond/branch_0_fun/pallas_call | solution.py:449
  30.9 71.5 %branch_0_fun.3 = bf16[40,65536]{1,0:T(8,128)(2,1)} custom-call(s32[512]{0:T(512)S(1)} %get-tuple-element.50.irrep_ref, s32[8,768]{1,0:T(8,128)S(1)} %get-tuple-element.52.slot_ref, bf16[40,768]{1,0:T(8,128)(2,1)S(1)} %bitcast.54, bf16[1,112,2048]{2,1,0:T(8,128)(2,1)S(1)} %branch_0_fun.2.mine_ref, bf16[40,65536]{1,0:T(8,128)(2,1)} %get-tuple-element.57.res_hbm), custom_call_target="tpu_custom_call" | custom-call | tf_op jit(solution)/shard_map/cond/branch_0_fun/pallas_call | solution.py:343
  102.6 5.2 %copy.51 = bf16[40,65536]{1,0:T(8,128)(2,1)} copy(bf16[40,65536]{1,0:T(8,128)(2,1)} %get-tuple-element.72) | data formatting | bytes 10485760
  (4 shorter events, 0.0 us)

commit v5 on v4

--- a/solution.py
+++ b/solution.py
@@ -135,7 +135,7 @@
 ):
     n_row, n_col = 8, 4
     row, z = lax.axis_index("row"), lax.axis_index("col")
-    rows = amps.shape[2]
+    pairs, padded, rows = amp_ref.shape[0], amps.shape[1], amps.shape[2]
     half = round_up(rows // 2, 16)
     along_rows = rows - 32
     along_part = pl.ds(0, along_rows)
@@ -186,11 +186,15 @@
             r = r_first + i * (r_other - r_first)
             chunk = order[j] * n_row + r
             slot = r * n_col + order[j]
-            for t in range(per_step):
-                g = irrep_ref[chunk * per_step + t]
-                cols = pl.ds(pl.multiple_of((chunk * per_step + t) * GRAIN, GRAIN), GRAIN)
-                piece = held[slot, :, t * GRAIN:(t + 1) * GRAIN]
-                ladder = jnp.dot(amps[g], piece, preferred_element_type=jnp.float32)
+            for t in range(0, per_step, 2):
+                block = chunk * per_step + t
+                two = jnp.concatenate([amps[irrep_ref[block]], amps[irrep_ref[block + 1]]], axis=0)
+                cols = pl.ds(pl.multiple_of(block * GRAIN, 2 * GRAIN), 2 * GRAIN)
+                piece = held[slot, :, t * GRAIN:(t + 2) * GRAIN]
+                both = jnp.dot(two, piece, preferred_element_type=jnp.float32)
+                ladder = jnp.concatenate(
+                    [both[:pairs, :GRAIN], both[padded:padded + pairs, GRAIN:]], axis=1
+                )
                 ladder = ladder.astype(jnp.bfloat16).astype(jnp.float32)
                 total = res_ref[:, cols].astype(jnp.float32) + ladder
                 out_ref[:, cols] = total.astype(jnp.bfloat16)
@@ -293,9 +297,10 @@
     pl.semaphore_wait(barrier, 4 + middle)
 
     own(0)
+    amps[...] = jnp.zeros_like(amps)
     for g in range(NIRREP):
         pick = one_hot_rows(slot_ref, g, rows)
-        amps[g] = lax.dot_general(
+        amps[g, :pairs, :] = lax.dot_general(
             amp_ref[...], pick, (((1,), (1,)), ((), ())), preferred_element_type=jnp.float32
         ).astype(jnp.bfloat16)
     reading.wait()
@@ -346,7 +351,7 @@
         in_specs=[pl.BlockSpec(memory_space=pltpu.SMEM), vmem, vmem, vmem, hbm],
         out_specs=hbm,
         scratch_shapes=[
-            pltpu.VMEM((NIRREP, amp.shape[0], rows), jnp.bfloat16),
+            pltpu.VMEM((NIRREP, round_up(amp.shape[0], 16), rows), jnp.bfloat16),
             pltpu.VMEM((parts, rows, width), jnp.bfloat16),
             pltpu.VMEM(residual.shape, jnp.bfloat16),
             pltpu.VMEM(residual.shape, jnp.bfloat16),

time: 115 us -> 115 us (level)
  no operation moved by 1% of the time
where the time goes in v5:
time: 115 us
  Pallas kernels  87.9 us (76%)
  between operations  15.3 us (13%)
  local copies, waits for them, and re-layouts  8.04 us (7%)
  matrix products  2.16 us (2%)
    pallas_call x1, Pallas kernels, spread_add(): pl.pallas_call(functools.partial(spread_kernel, per_step=width // GRAIN),...  71.4 us
    pallas_call x1, Pallas kernels, exchange(): pl.pallas_call(functools.partial(exchange_kernel, n_row=n_row, per_step=w...  16.5 us
    unnamed x1, local copies, waits for them, and re-layouts  5.18 us

profile of v5, /device:TPU:0, one launch (start us, length us, event | category | flops | bytes accessed | tf_op | source)
XLA Modules:
  0.0 114.5 jit_solution(11472661584079443618)
XLA Ops:
  6.5 0.7 slice.47
  7.3 0.1 convert_reduce_fusion.1
  7.4 0.7 eq.56
  8.1 0.1 lt.32
  8.1 2.2 %convolution_convert_fusion = s32[8,1552]{1,0:T(8,128)S(1)} fusion(bf16[768,1552]{1,0:T(8,128)(2,1)} %constant.48.clone, s32[768]{0:T(1024)S(1)} %eq.56), kind=kOutput, calls=%fused_computation.31 | convolution fusion | flops 19089536 | bytes 2436608 | tf_op jit(solution)/shard_map/dot_general | solution.py:493
  10.3 0.7 add_reduce_fusion
  13.0 0.1 lt.34
  13.0 0.1 lt.35
  13.1 0.1 add.53
  13.2 0.1 add.54
  13.3 0.1 reshape.44
  13.4 0.1 dynamic-slice_reduce_fusion
  13.4 0.1 reshape.45
  13.5 89.0 %conditional.1 = (bf16[40,65536]{1,0:T(8,128)(2,1)}) conditional(s32[]{:T(128)} %clamp.3, (bf16[40,3,256]{2,0,1:T(8,128)(2,1)}, s32[512]{0:T(512)S(1)}, s32[8,96]{1,0:T(8,128)S(1)}, s32[8,256]{1,0:T(8,128)S(1)}, bf16[3,32,16384]{2,1,0:T(8,128)(2,1)}, /*index=5*/s32[8,768]{1,0:T(8,128)S(1)}, bf16[40,65536]{1,0:T(8,128)(2,1)}) %tuple.14, ...), branch_computations={%region_3.4_spmd, %region_4.5_spmd, %region_5.7_spmd} | conditional | flops 4070391808 | bytes 227321024 | solution.py:538
  13.5 0.8 copy.44
  14.4 16.5 %branch_0_fun.2.mine_ref = bf16[1,112,2048]{2,1,0:T(8,128)(2,1)S(1)} custom-call(s32[512]{0:T(512)S(1)} %get-tuple-element.50.irrep_ref, s32[8,96]{1,0:T(8,128)S(1)} %get-tuple-element.54.slot1_ref, s32[8,256]{1,0:T(8,128)S(1)} %get-tuple-element.55.slot2_ref, bf16[3,32,16384]{2,1,0:T(8,128)(2,1)} %get-tuple-element.56.x_ref), custom_call_target="tpu_custom_call" | custom-call | tf_op jit(solution)/shard_map/cond/branch_0_fun/pallas_call | solution.py:454
  30.9 71.4 %branch_0_fun.3 = bf16[40,65536]{1,0:T(8,128)(2,1)} custom-call(s32[512]{0:T(512)S(1)} %get-tuple-element.50.irrep_ref, s32[8,768]{1,0:T(8,128)S(1)} %get-tuple-element.52.slot_ref, bf16[40,768]{1,0:T(8,128)(2,1)S(1)} %bitcast.54, bf16[1,112,2048]{2,1,0:T(8,128)(2,1)S(1)} %branch_0_fun.2.mine_ref, bf16[40,65536]{1,0:T(8,128)(2,1)} %get-tuple-element.57.res_hbm), custom_call_target="tpu_custom_call" | custom-call | tf_op jit(solution)/shard_map/cond/branch_0_fun/pallas_call | solution.py:348
  102.5 5.2 %copy.51 = bf16[40,65536]{1,0:T(8,128)(2,1)} copy(bf16[40,65536]{1,0:T(8,128)(2,1)} %get-tuple-element.72) | data formatting | bytes 10485760
  (4 shorter events, 0.0 us)

commit v6 on v5

--- a/solution.py
+++ b/solution.py
@@ -304,27 +304,27 @@
             amp_ref[...], pick, (((1,), (1,)), ((), ())), preferred_element_type=jnp.float32
         ).astype(jnp.bfloat16)
     reading.wait()
+    near(0)
+    own(1)
     own_done(0)
-    own(1)
-    near(0)
-    own_done(1)
+    diagonal(0)
     own(2)
     near(1)
+    own_done(1)
     near_done(0)
-    diagonal(0)
+    along(1)
     own(3)
+    diagonal_done(0)
     own_done(2)
-    near_done(1)
-    along(1)
     near(2)
-    diagonal_done(0)
-    own_done(3)
     along(2)
     diagonal(1)
-    near_done(2)
+    near_done(1)
+    own_done(3)
     near(3)
     along(3)
     diagonal(2)
+    near_done(2)
     diagonal_done(1)
     diagonal(3)
     near_done(3)

time: 115 us -> 116 us (level)
  no operation moved by 1% of the time
where the time goes in v6:
time: 116 us
  Pallas kernels  88.9 us (77%)
  between operations  15.3 us (13%)
  local copies, waits for them, and re-layouts  8.04 us (7%)
  matrix products  2.16 us (2%)
    pallas_call x1, Pallas kernels, spread_add(): pl.pallas_call(functools.partial(spread_kernel, per_step=width // GRAIN),...  72.4 us
    pallas_call x1, Pallas kernels, exchange(): pl.pallas_call(functools.partial(exchange_kernel, n_row=n_row, per_step=w...  16.5 us
    unnamed x1, local copies, waits for them, and re-layouts  5.18 us

profile of v6, /device:TPU:0, one launch (start us, length us, event | category | flops | bytes accessed | tf_op | source)
XLA Modules:
  0.0 115.5 jit_solution(17827643516358908463)
XLA Ops:
  6.5 0.7 slice.47
  7.3 0.1 convert_reduce_fusion.1
  7.4 0.7 eq.56
  8.1 0.1 lt.32
  8.1 2.2 %convolution_convert_fusion = s32[8,1552]{1,0:T(8,128)S(1)} fusion(bf16[768,1552]{1,0:T(8,128)(2,1)} %constant.48.clone, s32[768]{0:T(1024)S(1)} %eq.56), kind=kOutput, calls=%fused_computation.31 | convolution fusion | flops 19089536 | bytes 2436608 | tf_op jit(solution)/shard_map/dot_general | solution.py:493
  10.3 0.7 add_reduce_fusion
  13.0 0.1 lt.34
  13.0 0.1 lt.35
  13.1 0.1 add.53
  13.2 0.1 add.54
  13.3 0.1 reshape.44
  13.4 0.1 dynamic-slice_reduce_fusion
  13.4 0.1 reshape.45
  13.5 90.0 %conditional.1 = (bf16[40,65536]{1,0:T(8,128)(2,1)}) conditional(s32[]{:T(128)} %clamp.3, (bf16[40,3,256]{2,0,1:T(8,128)(2,1)}, s32[512]{0:T(512)S(1)}, s32[8,96]{1,0:T(8,128)S(1)}, s32[8,256]{1,0:T(8,128)S(1)}, bf16[3,32,16384]{2,1,0:T(8,128)(2,1)}, /*index=5*/s32[8,768]{1,0:T(8,128)S(1)}, bf16[40,65536]{1,0:T(8,128)(2,1)}) %tuple.14, ...), branch_computations={%region_3.4_spmd, %region_4.5_spmd, %region_5.7_spmd} | conditional | flops 4070391808 | bytes 227321024 | solution.py:538
  13.5 0.8 copy.44
  14.4 16.5 %branch_0_fun.2.mine_ref = bf16[1,112,2048]{2,1,0:T(8,128)(2,1)S(1)} custom-call(s32[512]{0:T(512)S(1)} %get-tuple-element.50.irrep_ref, s32[8,96]{1,0:T(8,128)S(1)} %get-tuple-element.54.slot1_ref, s32[8,256]{1,0:T(8,128)S(1)} %get-tuple-element.55.slot2_ref, bf16[3,32,16384]{2,1,0:T(8,128)(2,1)} %get-tuple-element.56.x_ref), custom_call_target="tpu_custom_call" | custom-call | tf_op jit(solution)/shard_map/cond/branch_0_fun/pallas_call | solution.py:454
  30.9 72.4 %branch_0_fun.3 = bf16[40,65536]{1,0:T(8,128)(2,1)} custom-call(s32[512]{0:T(512)S(1)} %get-tuple-element.50.irrep_ref, s32[8,768]{1,0:T(8,128)S(1)} %get-tuple-element.52.slot_ref, bf16[40,768]{1,0:T(8,128)(2,1)S(1)} %bitcast.54, bf16[1,112,2048]{2,1,0:T(8,128)(2,1)S(1)} %branch_0_fun.2.mine_ref, bf16[40,65536]{1,0:T(8,128)(2,1)} %get-tuple-element.57.res_hbm), custom_call_target="tpu_custom_call" | custom-call | tf_op jit(solution)/shard_map/cond/branch_0_fun/pallas_call | solution.py:348
  103.5 5.2 %copy.51 = bf16[40,65536]{1,0:T(8,128)(2,1)} copy(bf16[40,65536]{1,0:T(8,128)(2,1)} %get-tuple-element.72) | data formatting | bytes 10485760
  (4 shorter events, 0.0 us)
